TPU v7x, 256 devices: a whole 4x4x8 slice. The times are simulated.
256 devices in a mesh: row: 16 (over z, core), col: 4 (over y), rep: 4 (over x).
Axes of the slice: x: 4, y: 4, z: 8, core: 2. Of those that a mesh axis runs over, the one named last changes fastest.
Arguments:
- density: bfloat16 [8192, 8192], P('row', 'col'), may hold values from -1.5 to 1.75, as said below
- pattern_density: int32 [256, 256], P('row', 'col'), may hold values 0 or 1
- pattern_square: int32 [256, 256], P('row', 'col'), may hold values 0 or 1
- pattern_cube: int32 [256, 256], P('row', 'col'), may hold values 0 or 1
Outputs:
- purified: bfloat16 [8192, 8192], P('row', ('col', 'rep'))
Inputs may be any that keep to these rules, and one draw needn't show every extreme that they name: `density`: symmetric.
All inputs are finite; a program needn't handle non-finite values. No bound on the sum of `pattern_density` or of `pattern_square` or of `pattern_cube` on one device may be relied on, other than what follows from the above.
Results may differ from a plain program's by a relative error of at most 0.0054.
Values may be sent and summed in bfloat16 or wider, within the bound.
No kernel may reach another device: no remote copies, remote signals or barrier semaphores. Data moves between devices by JAX's collectives and lax.ppermute only.
A program may use at most 64 MiB of HBM per device.

v0:
```python
import jax
import jax.numpy as jnp
from jax import lax
from jax.sharding import PartitionSpec as P

BLK = 32


def spread(pattern, block_width):
    blocks_down, blocks_across = pattern.shape
    wide = jnp.broadcast_to(
        pattern[:, None, :, None] > 0, (blocks_down, block_width, blocks_across, block_width)
    )
    return wide.reshape(blocks_down * block_width, blocks_across * block_width)


def column_share(matrix, rep_depth, rep_layer, block_width):
    tile_rows, tile_width = matrix.shape
    shaped = matrix.reshape(
        tile_rows, tile_width // (rep_depth * block_width), rep_depth, block_width
    )
    picked = lax.dynamic_index_in_dim(shaped, rep_layer, 2, keepdims=False)
    return picked.reshape(tile_rows, tile_width // rep_depth)


def row_share(matrix, rep_depth, rep_layer, block_width):
    tile_rows, tile_width = matrix.shape
    shaped = matrix.reshape(
        tile_rows // (rep_depth * block_width), rep_depth, block_width, tile_width
    )
    picked = lax.dynamic_index_in_dim(shaped, rep_layer, 1, keepdims=False)
    return picked.reshape(tile_rows // rep_depth, tile_width)


def body(density, pattern_density, pattern_square, pattern_cube):
    tile_rows, tile_width = density.shape
    rep_depth = lax.axis_size("rep")
    rep_layer = lax.axis_index("rep")
    share_width = tile_width // rep_depth
    share_start = rep_layer * share_width
    masked = jnp.where(spread(pattern_density, BLK), density, jnp.zeros_like(density))
    right_share = row_share(masked, rep_depth, rep_layer, BLK)
    left_band = lax.all_gather(
        column_share(masked, rep_depth, rep_layer, BLK), "col", axis=1, tiled=True
    )
    right_band = lax.all_gather(right_share, "row", axis=0, tiled=True)
    product_one = jnp.dot(left_band, right_band, preferred_element_type=jnp.float32)
    square_keep = spread(pattern_square, BLK)
    summed = lax.psum(product_one, "rep")
    square = jnp.where(square_keep, summed, jnp.float32(0.0)).astype(jnp.bfloat16)
    left_square = lax.all_gather(
        column_share(square, rep_depth, rep_layer, BLK), "col", axis=1, tiled=True
    )
    product_two = jnp.dot(left_square, right_band, preferred_element_type=jnp.float32)
    cube_share = lax.psum_scatter(product_two, "rep", scatter_dimension=1, tiled=True)
    cube_keep = lax.dynamic_slice_in_dim(spread(pattern_cube, BLK), share_start, share_width, 1)
    square_cols = lax.dynamic_slice_in_dim(square, share_start, share_width, 1).astype(jnp.float32)
    cube = jnp.where(cube_keep, cube_share, jnp.float32(0.0))
    return (3.0 * square_cols - 2.0 * cube).astype(jnp.bfloat16)


def solution(mesh):
    placed = (P("row", "col"), P("row", "col"), P("row", "col"), P("row", "col"))
    return jax.shard_map(
        body, mesh=mesh, in_specs=placed, out_specs=P("row", ("col", "rep")), check_vma=False
    )
```

profile of v0, /device:TPU:1, one launch (start us, length us, event | category | flops | bytes accessed | tf_op | source)
XLA Modules:
  0.0 318.8 jit_solution(17400307454804896158)
XLA Ops:
  6.5 0.0 all-gather.4.cloned.1.call-start
  6.5 0.7 broadcast_compare_fusion.1
  7.2 3.1 broadcast_in_dim.30
  10.3 10.4 %reshape.37 = pred[512,2048]{1,0:T(8,128)(4,1)S(1)} reshape(pred[16,32,64,32]{3,2,1,0:T(8,128)(4,1)} %broadcast_in_dim.30) | data formatting | bytes 2097152 | tf_op jit(solution)/shard_map/reshape | solution.py:14
  20.7 1.8 broadcast_select_fusion
  22.5 2.5 copy.5
  25.0 1.9 constant_dynamic-slice_fusion.2
  26.9 0.0 all-gather.4.cloned.1.call-update
  27.0 0.0 all-gather.6.cloned.1.call-start
  27.0 0.9 constant_dynamic-slice_fusion.1
  27.9 0.0 all-gather.6.cloned.1.call-update
  27.9 0.0 all-gather.8.cloned.1.call-start
  27.9 0.0 copy-done
  28.0 3.1 broadcast_in_dim.15
  31.1 10.4 %reshape.36 = pred[512,2048]{1,0:T(8,128)(4,1)S(1)} reshape(pred[16,32,64,32]{3,2,1,0:T(8,128)(4,1)} %broadcast_in_dim.15) | data formatting | bytes 2097152 | tf_op jit(solution)/shard_map/reshape | solution.py:14
  41.4 22.9 %all-gather.4.cloned.1.call-done = bf16[512,2048]{0,1:T(8,128)(2,1)} async-done(((bf16[512,512]{0,1:T(8,128)(2,1)}), bf16[512,2048]{0,1:T(8,128)(2,1)}) %all-gather.4.cloned.1.call-update) | async-done | bytes 2097168 | tf_op jit(solution)/shard_map/all_gather | solution.py:43
  64.3 58.2 %all-gather.6.cloned.1.call-done = bf16[2048,2048]{1,0:T(8,128)(2,1)} async-done(((bf16[128,2048]{1,0:T(8,128)(2,1)}), bf16[2048,2048]{1,0:T(8,128)(2,1)}) %all-gather.6.cloned.1.call-update) | async-done | bytes 8388624 | tf_op jit(solution)/shard_map/all_gather | solution.py:46
  122.5 10.5 %fusion = f32[512,2048]{1,0:T(8,128)} fusion(bf16[512,2048]{0,1:T(8,128)(2,1)} %all-gather.4.cloned.1.call-done, bf16[2048,2048]{1,0:T(8,128)(2,1)} %all-gather.6.cloned.1.call-done), kind=kOutput, calls=%fused_computation.9 | convolution fusion | flops 4294967296 | bytes 14680064 | tf_op jit(solution)/shard_map/dot_general | solution.py:47
  133.1 78.3 %all-reduce.1 = bf16[512,2048]{1,0:T(8,128)(2,1)} all-reduce(f32[512,2048]{1,0:T(8,128)} %fusion), channel_id=1, replica_groups=mesh['row'=16,'col'=4,'rep'=4] {'rep'}, use_global_device_ids=true, to_apply=%region_0.1 | all-reduce | flops 1048576 | bytes 6291456 | tf_op jit(solution)/shard_map/psum | solution.py:49
  211.4 2.3 select_convert_fusion
  213.7 2.6 copy.6
  216.3 1.9 constant_dynamic-slice_fusion
  218.1 0.0 all-gather.8.cloned.1.call-update
  218.2 0.2 reduce-scatter.2.cloned.1.call-start
  218.4 31.4 %all-gather.8.cloned.1.call-done = bf16[512,2048]{0,1:T(8,128)(2,1)} async-done(((bf16[512,512]{0,1:T(8,128)(2,1)}), bf16[512,2048]{0,1:T(8,128)(2,1)}) %all-gather.8.cloned.1.call-update) | async-done | bytes 2097168 | tf_op jit(solution)/shard_map/all_gather | solution.py:51
  249.8 10.5 %fusion.1 = f32[512,2048]{1,0:T(8,128)} fusion(bf16[512,2048]{0,1:T(8,128)(2,1)} %all-gather.8.cloned.1.call-done, bf16[2048,2048]{1,0:T(8,128)(2,1)} %all-gather.6.cloned.1.call-done), kind=kOutput, calls=%fused_computation.10 | convolution fusion | flops 4294967296 | bytes 14680064 | tf_op jit(solution)/shard_map/dot_general | solution.py:54
  260.3 0.0 reduce-scatter.2.cloned.1.call-update
  260.3 0.7 copy-done.1
  261.0 3.1 broadcast_in_dim.33
  264.1 10.5 %reshape.42 = pred[512,2048]{1,0:T(8,128)(4,1)S(1)} reshape(pred[16,32,64,32]{3,2,1,0:T(8,128)(4,1)} %broadcast_in_dim.33) | data formatting | bytes 2097152 | tf_op jit(solution)/shard_map/reshape | solution.py:14
  274.6 35.3 %reduce-scatter.2.cloned.1.call-done = f32[512,512]{1,0:T(8,128)} async-done(((f32[512,2048]{1,0:T(8,128)}), f32[512,512]{1,0:T(8,128)}) %reduce-scatter.2.cloned.1.call-update) | async-done | bytes 1048592 | tf_op jit(solution)/shard_map/reduce_scatter | solution.py:55
  309.9 2.3 subtract_convert_fusion
  (4 shorter events, 0.0 us)
Async XLA Ops:
  6.5 57.8 %all-gather.4.cloned.1.call-start = ((), (), s32[]{:S(2)}) async-start(), calls=%async_computation.1 | async-start | bytes 2621440 | tf_op jit(solution)/shard_map/all_gather | solution.py:43
  25.0 2.9 copy-start
  27.0 95.6 %all-gather.6.cloned.1.call-start = ((), (), s32[]{:S(2)}) async-start(), calls=%async_computation.2 | async-start | bytes 8912896 | tf_op jit(solution)/shard_map/all_gather | solution.py:46
  27.9 221.9 %all-gather.8.cloned.1.call-start = ((), (), s32[]{:S(2)}) async-start(), calls=%async_computation.3 | async-start | bytes 2621440 | tf_op jit(solution)/shard_map/all_gather | solution.py:51
  218.2 91.7 %reduce-scatter.2.cloned.1.call-start = ((), (), s32[]{:S(2)}) async-start(), calls=%async_computation.4 | async-start | bytes 5242880 | tf_op jit(solution)/shard_map/reduce_scatter | solution.py:55
  260.3 0.7 copy-start.1
Sparse Core Ops, SparseCore 0:
  27.1 37.2 all-gather.3
  66.1 56.3 all-gather.5
  218.3 31.4 all-gather.7
  260.5 49.4 reduce-scatter.1
where the time goes:
time: 320 us; the launch traced here: 319 us
  waiting for transfers between devices  148 us (46%)
  blocking collectives  78.3 us (24%)
  local copies, waits for them, and re-layouts  50.9 us (16%)
  matrix products  21.1 us (7%)
  between operations  13.2 us (4%)
  other arithmetic  7.09 us (2%)
    psum x1, blocking collectives, body(): summed = lax.psum(product_one, 'rep')  78.3 us
    all_gather x1, waiting for transfers between devices, body(): right_band = lax.all_gather(right_share, 'row', axis=0, tiled=True)  58.2 us
    reduce_scatter x1, waiting for transfers between devices, body(): lax.psum_scatter(product_two, 'rep', scatter_dimension=1, tiled=True)  35.3 us
    all_gather x1, waiting for transfers between devices, body(): lax.all_gather(column_share(square, rep_depth, rep_layer, BLK), 'col', ax...  31.4 us
    reshape x3, local copies, waits for them, and re-layouts, spread(): return wide.reshape(blocks_down * block_width, blocks_across * block_width)  31.3 us
    all_gather x1, waiting for transfers between devices, body(): lax.all_gather(column_share(masked, rep_depth, rep_layer, BLK), 'col', ax...  22.9 us
    dot_general x1, matrix products, body(): jnp.dot(left_square, right_band, preferred_element_type=jnp.float32)  10.5 us
    dot_general x1, matrix products, body(): jnp.dot(left_band, right_band, preferred_element_type=jnp.float32)  10.5 us
  transfers between devices with their start and end apart: 4, of which 4 were waited for; matrix products, arithmetic and copies ran while one was open for 9% of the time, Pallas kernels for 0%

commit v1 on v0

--- a/solution.py
+++ b/solution.py
@@ -1,9 +1,17 @@
+import functools
 import jax
 import jax.numpy as jnp
 from jax import lax
 from jax.sharding import PartitionSpec as P
 
 BLK = 32
+
+
+def close_floor(field, group_axis):
+    return jnp.sum(lax.all_gather(field, group_axis), axis=0)
+
+
+make_the_pieces_all = functools.partial(close_floor, group_axis="rep")
 
 
 def spread(pattern, block_width):
@@ -46,7 +54,7 @@
     right_band = lax.all_gather(right_share, "row", axis=0, tiled=True)
     product_one = jnp.dot(left_band, right_band, preferred_element_type=jnp.float32)
     square_keep = spread(pattern_square, BLK)
-    summed = lax.psum(product_one, "rep")
+    summed = make_the_pieces_all(product_one)
     square = jnp.where(square_keep, summed, jnp.float32(0.0)).astype(jnp.bfloat16)
     left_square = lax.all_gather(
         column_share(square, rep_depth, rep_layer, BLK), "col", axis=1, tiled=True

time: 320 us -> 405 us (1.27)
  waiting for transfers between devices: 148 us -> 304 us
  blocking collectives: 78.3 us -> 0 us
  other arithmetic: 7.09 us -> 15 us
    all_gather x0 -> x1, waiting for transfers between devices: none -> 154 us  [close_floor(): return jnp.sum(lax.all_gather(field, group_axis), axis=0)]
    psum x1 -> x0, blocking collectives: 78.3 us -> none  [body(): summed = lax.psum(product_one, 'rep')]
    reduce_scatter x1, waiting for transfers between devices: 35.3 us -> 21.6 us  [body(): lax.psum_scatter(product_two, 'rep', scatter_dimension=1, tiled=True)]
    all_gather x1, waiting for transfers between devices: 22.9 us -> 36.4 us  [body(): lax.all_gather(column_share(masked, rep_depth, rep_layer, BLK), 'col', ax...]
    reduce_sum x0 -> x1, other arithmetic: none -> 8.11 us  [close_floor(): return jnp.sum(lax.all_gather(field, group_axis), axis=0)]
    broadcast_in_dim x3 -> x5, local copies, waits for them, and re-layouts: 9.28 us -> 9.8 us  [spread(): jnp.broadcast_to(pattern[:, None, :, None] > 0, (blocks_down, block_width...]
  transfers between devices with their start and end apart: 4 -> 5, of which waited for: 4 -> 5; matrix products, arithmetic and copies ran while one was open for 9% -> 7% of each run, Pallas kernels for 0% -> 0%
where the time goes in v1:
time: 405 us; the launch traced here: 404 us
  waiting for transfers between devices  304 us (75%)
  local copies, waits for them, and re-layouts  50.4 us (12%)
  matrix products  21.1 us (5%)
  other arithmetic  15 us (4%)
  between operations  13.2 us (3%)
    all_gather x1, waiting for transfers between devices, close_floor(): return jnp.sum(lax.all_gather(field, group_axis), axis=0)  154 us
    all_gather x1, waiting for transfers between devices, body(): right_band = lax.all_gather(right_share, 'row', axis=0, tiled=True)  58.2 us
    all_gather x1, waiting for transfers between devices, body(): lax.all_gather(column_share(masked, rep_depth, rep_layer, BLK), 'col', ax...  36.4 us
    all_gather x1, waiting for transfers between devices, body(): lax.all_gather(column_share(square, rep_depth, rep_layer, BLK), 'col', ax...  34.3 us
    reshape x3, local copies, waits for them, and re-layouts, spread(): return wide.reshape(blocks_down * block_width, blocks_across * block_width)  32 us
    reduce_scatter x1, waiting for transfers between devices, body(): lax.psum_scatter(product_two, 'rep', scatter_dimension=1, tiled=True)  21.6 us
    dot_general x1, matrix products, body(): jnp.dot(left_band, right_band, preferred_element_type=jnp.float32)  10.5 us
    dot_general x1, matrix products, body(): jnp.dot(left_square, right_band, preferred_element_type=jnp.float32)  10.5 us
  transfers between devices with their start and end apart: 5, of which 5 were waited for; matrix products, arithmetic and copies ran while one was open for 7% of the time, Pallas kernels for 0%

profile of v1, /device:TPU:1, one launch (start us, length us, event | category | flops | bytes accessed | tf_op | source)
XLA Modules:
  0.0 404.3 jit_solution(6327701106821798454)
XLA Ops:
  6.5 0.7 broadcast_compare_fusion.1
  7.2 3.1 broadcast_in_dim.38
  10.3 10.4 %reshape.38 = pred[512,2048]{1,0:T(8,128)(4,1)S(1)} reshape(pred[16,32,64,32]{3,2,1,0:T(8,128)(4,1)} %broadcast_in_dim.38) | data formatting | bytes 2097152 | tf_op jit(solution)/shard_map/reshape | solution.py:22
  20.7 1.8 broadcast_select_fusion
  22.5 2.5 copy.5
  25.1 1.9 constant_dynamic-slice_fusion.2
  26.9 0.0 all-gather.6.cloned.1.call-update
  27.0 0.0 all-gather.8.cloned.1.call-start
  27.0 0.8 constant_dynamic-slice_fusion.1
  27.9 0.0 all-gather.12.cloned.1.call-start
  27.9 36.4 %all-gather.6.cloned.1.call-done = bf16[512,2048]{0,1:T(8,128)(2,1)} async-done(((bf16[512,512]{0,1:T(8,128)(2,1)}), bf16[512,2048]{0,1:T(8,128)(2,1)}) %all-gather.6.cloned.1.call-update) | async-done | bytes 2097168 | tf_op jit(solution)/shard_map/all_gather | solution.py:51
  64.3 58.2 %all-gather.8.cloned.1.call-done = bf16[2048,2048]{1,0:T(8,128)(2,1)} async-done(((bf16[128,2048]{1,0:T(8,128)(2,1)}), bf16[2048,2048]{1,0:T(8,128)(2,1)}) %all-gather.8.cloned.1.call-update) | async-done | bytes 8388624 | tf_op jit(solution)/shard_map/all_gather | solution.py:54
  122.5 10.5 %fusion.2 = f32[512,2048]{1,0:T(8,128)} fusion(bf16[512,2048]{0,1:T(8,128)(2,1)} %all-gather.6.cloned.1.call-done, bf16[2048,2048]{1,0:T(8,128)(2,1)} %all-gather.8.cloned.1.call-done), kind=kOutput, calls=%fused_computation.12 | convolution fusion | flops 4294967296 | bytes 14680064 | tf_op jit(solution)/shard_map/dot_general | solution.py:55
  133.1 0.0 all-gather.10.cloned.1.call-start
  133.2 0.6 copy-done
  133.8 0.1 copy.6
  133.9 0.2 broadcast_in_dim.42
  134.1 0.3 broadcast_in_dim.43
  134.4 0.1 constant_dynamic-slice_fusion
  134.4 153.6 %all-gather.12.cloned.1.call-done = f32[2048,2048]{1,0:T(8,128)} async-done(((f32[512,2048]{1,0:T(8,128)}), f32[2048,2048]{1,0:T(8,128)}) %all-gather.12.cloned.1.call-update) | async-done | bytes 16777232 | tf_op jit(solution)/shard_map/all_gather | solution.py:11
  288.1 8.1 %reduce_sum.11 = bf16[512,2048]{1,0:T(8,128)(2,1)S(1)} reduce(f32[4,512,2048]{2,1,0:T(8,128)} %bitcast.19, f32[]{:T(128)} %constant.8.clone.1), dimensions={0}, to_apply=%region_0.1 | reduce | flops 3145728 | bytes 18874372 | tf_op jit(solution)/shard_map/reduce_sum | solution.py:11
  296.2 2.5 copy.7
  298.7 2.0 fusion
  300.7 0.2 reduce-scatter.2.cloned.1.call-start
  300.9 34.3 %all-gather.10.cloned.1.call-done = bf16[512,2048]{0,1:T(8,128)(2,1)} async-done(((bf16[512,512]{0,1:T(8,128)(2,1)}), bf16[512,2048]{0,1:T(8,128)(2,1)}) %all-gather.10.cloned.1.call-update) | async-done | bytes 2097168 | tf_op jit(solution)/shard_map/all_gather | solution.py:59
  335.2 10.5 %fusion.3 = f32[512,2048]{1,0:T(8,128)} fusion(bf16[512,2048]{0,1:T(8,128)(2,1)} %all-gather.10.cloned.1.call-done, bf16[2048,2048]{1,0:T(8,128)(2,1)} %all-gather.8.cloned.1.call-done), kind=kOutput, calls=%fused_computation.13 | convolution fusion | flops 4294967296 | bytes 14680064 | tf_op jit(solution)/shard_map/dot_general | solution.py:62
  345.8 3.1 broadcast_in_dim.37
  348.9 10.5 %reshape.37 = pred[512,2048]{1,0:T(8,128)(4,1)S(1)} reshape(pred[16,32,64,32]{3,2,1,0:T(8,128)(4,1)} %broadcast_in_dim.37) | data formatting | bytes 2097152 | tf_op jit(solution)/shard_map/reshape | solution.py:22
  359.5 3.1 broadcast_in_dim.41
  362.6 11.2 %reshape.43 = pred[512,2048]{1,0:T(8,128)(4,1)} reshape(pred[16,32,64,32]{3,2,1,0:T(8,128)(4,1)} %broadcast_in_dim.41) | data formatting | bytes 2097152 | tf_op jit(solution)/shard_map/reshape | solution.py:22
  373.7 21.6 %reduce-scatter.2.cloned.1.call-done = f32[512,512]{1,0:T(8,128)} async-done(((f32[512,2048]{1,0:T(8,128)}), f32[512,512]{1,0:T(8,128)}) %reduce-scatter.2.cloned.1.call-update) | async-done | bytes 1048592 | tf_op jit(solution)/shard_map/reduce_scatter | solution.py:63
  395.4 2.4 subtract_convert_fusion
  (10 shorter events, 0.1 us)
Async XLA Ops:
  6.5 57.8 %all-gather.6.cloned.1.call-start = ((), (), s32[]{:S(2)}) async-start(), calls=%async_computation.1 | async-start | bytes 2621440 | tf_op jit(solution)/shard_map/all_gather | solution.py:51
  27.0 95.6 %all-gather.8.cloned.1.call-start = ((), (), s32[]{:S(2)}) async-start(), calls=%async_computation.2 | async-start | bytes 8912896 | tf_op jit(solution)/shard_map/all_gather | solution.py:54
  27.9 260.2 %all-gather.12.cloned.1.call-start = ((), (), s32[]{:S(2)}) async-start(), calls=%async_computation.5 | async-start | bytes 20971520 | tf_op jit(solution)/shard_map/all_gather | solution.py:11
  133.1 0.7 copy-start
  133.1 202.1 %all-gather.10.cloned.1.call-start = ((), (), s32[]{:S(2)}) async-start(), calls=%async_computation.3 | async-start | bytes 2621440 | tf_op jit(solution)/shard_map/all_gather | solution.py:59
  300.7 94.7 %reduce-scatter.2.cloned.1.call-start = ((), (), s32[]{:S(2)}) async-start(), calls=%async_computation.4 | async-start | bytes 5242880 | tf_op jit(solution)/shard_map/reduce_scatter | solution.py:63
  348.9 10.5 %copy-start.1 = (s32[16,64]{1,0:T(8,128)S(1)}, s32[16,64]{1,0:T(8,128)}, u32[]{:S(2)}) copy-start(s32[16,64]{1,0:T(8,128)} %param.7) | copy-start | bytes 12292
Sparse Core Ops, SparseCore 0:
  27.1 37.2 all-gather.5
  66.2 56.3 all-gather.7
  133.2 154.7 all-gather.11
  300.8 34.4 all-gather.9
  345.9 49.3 reduce-scatter.1
